TPU v7x, 512 devices: a whole 4x4x16 slice. The times are simulated.
512 devices in a mesh: own: 64 (over z, x), pair: 8 (over y, core).
Axes of the slice: x: 4, y: 4, z: 16, core: 2. Of those that a mesh axis runs over, the one named last changes fastest.
Arguments:
- points: bfloat16 [65536, 64], P(('own', 'pair')), may hold values from -6 to 6
- inv_scale: float32 [64], replicated, may hold values from 0.05 to 0.6
- tasks: int32 [65536], P(('own', 'pair')), may hold values from 0 to 7
- task_cov: float32 [8, 8], replicated, may hold values from -0.12 to 1.5, as said below
- solution: float32 [65536, 16], P(('own', 'pair')), may hold values from -6 to 6
- residual: float32 [65536, 16], P(('own', 'pair')), may hold values from -30 to 30
- direction: float32 [65536, 16], P(('own', 'pair')), may hold values from -30 to 30
Outputs:
- new_solution: float32 [65536, 16], P(('own', 'pair'))
- new_residual: float32 [65536, 16], P(('own', 'pair'))
- new_direction: float32 [65536, 16], P(('own', 'pair'))
Inputs may be any that keep to these rules, and one draw needn't show every extreme that they name: `task_cov`: symmetric, and each diagonal entry exceeds the sum of magnitudes of the other entries of its row.
All inputs are finite; a program needn't handle non-finite values.
Results may differ from a plain program's by a relative error of at most 0.0044.
Values may be sent and summed in bfloat16 or wider, within the bound.
No kernel may reach another device: no remote copies, remote signals or barrier semaphores. Data moves between devices by JAX's collectives and lax.ppermute only.
A program may use at most 128 MiB of HBM per device.

v0:
```python
import jax
import jax.numpy as jnp
from jax import lax
from jax.sharding import PartitionSpec as P

noise_var = 1.0


def body(points, inv_scale, tasks, task_cov, solution, residual, direction):
    shard_rows = points.shape[0]
    owners = lax.axis_size("own")
    owner_index = lax.axis_index("own")
    scaled = (points.astype(jnp.float32) * inv_scale).astype(jnp.bfloat16)
    dir_low = direction.astype(jnp.bfloat16)
    task_vals = tasks.astype(jnp.bfloat16)
    row_scaled, row_dir, row_task = (
        lax.all_gather(scaled, "pair", axis=0, tiled=True),
        lax.all_gather(dir_low, "pair", axis=0, tiled=True),
        lax.all_gather(task_vals, "pair", axis=0, tiled=True),
    )
    row_sq = jnp.sum(jnp.square(row_scaled.astype(jnp.float32)), axis=1)
    levels = task_cov.shape[0]
    labels = jnp.arange(levels).astype(jnp.float32)
    row_hot = (row_task.astype(jnp.float32)[:, None] == labels[None, :]).astype(jnp.float32)
    row_cov = jnp.dot(row_hot, task_cov, precision=lax.Precision.HIGHEST)
    row_count = row_scaled.shape[0]
    probes = direction.shape[1]

    def kernel_tile(col_scaled, col_task):
        inner_prod = lax.dot_general(
            row_scaled, col_scaled, (((1,), (1,)), ((), ())), preferred_element_type=jnp.float32
        )
        col_sq = jnp.sum(jnp.square(col_scaled.astype(jnp.float32)), axis=1)
        col_hot = (col_task.astype(jnp.float32)[:, None] == labels[None, :]).astype(jnp.float32)
        factor = lax.dot_general(
            row_cov, col_hot, (((1,), (1,)), ((), ())), precision=lax.Precision.HIGHEST
        )
        return (
            factor * jnp.exp(-0.5 * (row_sq[:, None] + col_sq[None, :] - 2.0 * inner_prod))
        ).astype(jnp.bfloat16)

    row_start = jnp.zeros((row_count, probes), jnp.float32)
    col_start = jnp.zeros((owners * shard_rows, probes), jnp.float32)
    col_scaled = lax.all_gather(scaled, "own", axis=0, tiled=True)
    col_dir = lax.all_gather(dir_low, "own", axis=0, tiled=True)
    col_task = lax.all_gather(task_vals, "own", axis=0, tiled=True)
    length = col_scaled.shape[0]
    owner_ids = jnp.arange(length) // shard_rows
    distance = (owner_ids - owner_index) % owners
    oriented = (distance >= owners - (owners - 1) // 2) & (distance <= owners - 1) | (
        owners % 2 == 0
    ) & (distance == owners // 2) & (owner_index < owners // 2)
    row_use = (distance == 0) | oriented

    def work(partial_value):
        kernel = kernel_tile(col_scaled, col_task)
        masked_dir = col_dir * row_use[:, None].astype(jnp.bfloat16)
        row_total = jnp.dot(kernel, masked_dir, preferred_element_type=jnp.float32)
        transposed = lax.dot_general(
            kernel, row_dir, (((0,), (0,)), ((), ())), preferred_element_type=jnp.float32
        )
        transposed = transposed * oriented[:, None].astype(jnp.float32)
        return (row_total, transposed)

    def keep(partial_value):
        return partial_value

    row_total, col_total = lax.cond(jnp.any(row_use), work, keep, (row_start, col_start))
    col_part = lax.psum_scatter(col_total, "own", scatter_dimension=0, tiled=True)
    row_part = lax.psum_scatter(row_total, "pair", scatter_dimension=0, tiled=True)
    product = row_part + col_part + noise_var * direction
    curve_local = jnp.sum(direction * product, axis=0)
    norm_local = jnp.sum(residual * residual, axis=0)
    curvature, norm_old = lax.psum((curve_local, norm_local), ("own", "pair"))
    step_size = norm_old / curvature
    new_residual = residual - step_size * product
    norm_new = lax.psum(jnp.sum(new_residual * new_residual, axis=0), ("own", "pair"))
    new_solution = solution + step_size * direction
    new_direction = new_residual + norm_new / norm_old * direction
    return (new_solution, new_residual, new_direction)


def solution(mesh):
    placed = (
        P(("own", "pair"), None),
        P(),
        P(("own", "pair")),
        P(),
        P(("own", "pair"), None),
        P(("own", "pair"), None),
        P(("own", "pair"), None),
    )
    return jax.shard_map(
        body,
        mesh=mesh,
        in_specs=placed,
        out_specs=(P(("own", "pair"), None), P(("own", "pair"), None), P(("own", "pair"), None)),
        check_vma=False,
    )
```

profile of v0, /device:TPU:1, one launch (start us, length us, event | category | flops | bytes accessed | tf_op | source)
XLA Modules:
  0.0 1008.1 jit_solution(16153451680494490864)
XLA Ops:
  7.2 0.8 copy.17
  8.1 1.3 multiply_convert_fusion
  9.4 19.8 %all_gather.20 = bf16[1024,64]{1,0:T(8,128)(2,1)S(1)} all-gather(bf16[128,64]{1,0:T(8,128)(2,1)} %multiply_convert_fusion), channel_id=1, replica_groups=mesh['own'=64,'pair'=8] {'pair'}, dimensions={0}, use_global_device_ids=true | all-gather | bytes 147456 | tf_op jit(solution)/shard_map/all_gather | solution.py:17
  29.2 0.7 convert_bitcast_fusion
  29.9 8.0 all-gather.1
  37.9 0.7 convert_element_type.56
  38.6 0.7 fusion.17
  39.9 67.6 %all-gather = bf16[64,1,128]{2,1,0:T(2,128)(2,1)S(1)} all-gather(bf16[1,1,128]{2,1,0:T(2,128)(2,1)S(1)} %convert_bitcast_fusion), channel_id=1, replica_groups=mesh['own'=64,'pair'=8] {'own'}, dimensions={0}, use_global_device_ids=true | all-gather | bytes 16640 | tf_op jit(solution)/shard_map/all_gather | solution.py:46
  107.5 20.8 %all_gather.23 = bf16[1024,16]{0,1:T(8,128)(2,1)S(1)} all-gather(bf16[128,16]{0,1:T(8,128)(2,1)S(1)} %convert_element_type.56), channel_id=1, replica_groups=mesh['own'=64,'pair'=8] {'pair'}, dimensions={0}, use_global_device_ids=true | all-gather | bytes 36864 | tf_op jit(solution)/shard_map/all_gather | solution.py:18
  128.3 73.4 %all_gather.22 = bf16[8192,16]{0,1:T(8,128)(2,1)S(1)} all-gather(bf16[128,16]{0,1:T(8,128)(2,1)S(1)} %convert_element_type.56), channel_id=1, replica_groups=mesh['own'=64,'pair'=8] {'own'}, dimensions={0}, use_global_device_ids=true | all-gather | bytes 266240 | tf_op jit(solution)/shard_map/all_gather | solution.py:45
  202.3 52.2 %conditional.1 = (f32[1024,16]{0,1:T(8,128)S(1)}, f32[8192,16]{0,1:T(8,128)S(1)}) conditional(s32[]{:T(128)} %convert_element_type.49, () %tuple.16, (bf16[64,1,128]{2,1,0:T(2,128)(2,1)S(1)}, f32[8]{0:T(128)S(1)}, f32[1024,8]{0,1:T(8,128)S(1)}, f32[1024,64]{1,0:T(8,128)S(1)}, bf16[8192,64]{1,0:T(8,128)(2,1)}, ...), branch_computations={%region_3.4_spmd, %region_4.7_spmd} | conditional | flops 2468297728 | bytes 192454768 | solution.py:68
  202.3 2.7 multiply_reduce_fusion
  205.2 17.4 %fusion.3 = f32[8192,1024]{1,0:T(8,128)} fusion(f32[1024,8]{0,1:T(8,128)S(1)} %get-tuple-element.25, f32[8192]{0:T(1024)S(1)} %bitcast_convert_fusion, f32[8]{0:T(128)S(1)} %get-tuple-element.24), kind=kOutput, calls=%fused_computation.7 | convolution fusion | flops 805371904 | bytes 33620000 | tf_op jit(solution)/shard_map/cond/branch_1_fun/dot_general | solution.py:35
  222.8 18.7 %fusion = bf16[1024,8192]{0,1:T(8,128)(2,1)} fusion(f32[8192,1024]{1,0:T(8,128)} %fusion.3, bf16[1024,64]{1,0:T(8,128)(2,1)S(1)} %get-tuple-element.28, bf16[8192,64]{1,0:T(8,128)(2,1)S(1)} %copy-done.2, f32[8192]{0:T(1024)S(1)} %multiply_reduce_fusion, f32[1024]{0:T(1024)S(1)} %multiply_reduce_fusion.1), kind=kOutput, calls=%fused_computation.1 | convolution fusion | flops 1124073472 | bytes 51548160 | tf_op jit(solution)/shard_map/cond/branch_1_fun/dot_general | solution.py:30
  241.6 10.4 %convolution_multiply_fusion = f32[8192,16]{0,1:T(8,128)S(1)} fusion(bf16[1024,8192]{0,1:T(8,128)(2,1)} %fusion, bf16[1024,16]{0,1:T(8,128)(2,1)S(1)} %get-tuple-element.31, f32[8192]{0:T(1024)S(1)} %convert_element_type.39), kind=kOutput, calls=%fused_computation.2 | convolution fusion | flops 268566528 | bytes 17367040 | tf_op jit(solution)/shard_map/cond/branch_1_fun/dot_general | solution.py:59
  252.1 2.3 fusion.1
  254.5 0.6 copy-done.4
  256.0 54.9 %reduce-scatter.3.cloned.1.call-done = f32[128,16]{0,1:T(8,128)} async-done(((f32[1024,16]{0,1:T(8,128)}), f32[128,16]{0,1:T(8,128)}) %reduce-scatter.3.cloned.1.call-update) | async-done | bytes 8208 | tf_op jit(solution)/shard_map/reduce_scatter | solution.py:70
  310.9 475.0 %reduce-scatter.5.cloned.1.call-done = f32[128,16]{0,1:T(8,128)} async-done(((f32[8192,16]{0,1:T(8,128)}), f32[128,16]{0,1:T(8,128)}) %reduce-scatter.5.cloned.1.call-update) | async-done | bytes 8208 | tf_op jit(solution)/shard_map/reduce_scatter | solution.py:69
  785.9 0.8 multiply_reduce_fusion.3
  786.7 113.3 %all-reduce = (f32[16]{0:T(128)S(1)}, f32[16]{0:T(128)S(1)}) all-reduce(f32[16]{0:T(128)S(1)} %multiply_reduce_fusion.4, f32[16]{0:T(128)S(1)} %multiply_reduce_fusion.3), channel_id=1, replica_groups=mesh['own'=64,'pair'=8] {'own','pair'}, use_global_device_ids=true, to_apply=%region_1.2 | all-reduce | flops 32 | bytes 256 | tf_op jit(solution)/shard_map/psum | solution.py:74
  900.0 1.5 multiply_reduce_fusion.2
  901.5 99.4 %psum.23 = f32[16]{0:T(128)S(1)} all-reduce(f32[16]{0:T(128)S(1)} %get-tuple-element.43), channel_id=1, replica_groups=mesh['own'=64,'pair'=8] {'own','pair'}, use_global_device_ids=true, to_apply=%region_12.13 | all-reduce | flops 16 | bytes 128 | tf_op jit(solution)/shard_map/psum | solution.py:77
  1000.9 0.7 multiply_add_fusion
  (37 shorter events, 2.0 us)
Async XLA Ops:
  7.2 194.6 %copy-start = (f32[8,8]{1,0:T(8,128)S(1)}, f32[8,8]{1,0:T(8,128)}, u32[]{:S(2)}) copy-start(f32[8,8]{1,0:T(8,128)} %param.12) | copy-start | bytes 772
  7.2 195.1 %all-gather.4.cloned.1.call-start = ((), (), s32[]{:S(2)}) async-start(), calls=%async_computation.2 | async-start | bytes 2129920 | tf_op jit(solution)/shard_map/all_gather | solution.py:44
  9.4 301.5 %reduce-scatter.3.cloned.1.call-start = ((), (), s32[]{:S(2)}) async-start(), calls=%async_computation.3 | async-start | bytes 73728 | tf_op jit(solution)/shard_map/reduce_scatter | solution.py:70
  202.3 53.6 %copy-start.7 = (f32[128,16]{0,1:T(8,128)S(1)}, f32[128,16]{0,1:T(8,128)}, u32[]{:S(2)}) copy-start(f32[128,16]{0,1:T(8,128)} %param.14) | copy-start | bytes 24580
  202.3 583.6 %copy-start.5 = (f32[128,16]{0,1:T(8,128)S(1)}, f32[128,16]{0,1:T(8,128)}, u32[]{:S(2)}) copy-start(f32[128,16]{0,1:T(8,128)} %param.15) | copy-start | bytes 24580
  202.3 697.7 %copy-start.8 = (f32[128,16]{0,1:T(8,128)S(1)}, f32[128,16]{0,1:T(8,128)}, u32[]{:S(2)}) copy-start(f32[128,16]{0,1:T(8,128)} %param.13) | copy-start | bytes 24580
  205.2 17.6 %copy-start.2 = (bf16[8192,64]{1,0:T(8,128)(2,1)S(1)}, bf16[8192,64]{1,0:T(8,128)(2,1)}, u32[]{:S(2)}) copy-start(bf16[8192,64]{1,0:T(8,128)(2,1)} %get-tuple-element.27) | copy-start | bytes 3145732 | tf_op jit(solution)/shard_map/cond
  241.5 10.5 %copy-start.1 = (bf16[1024,8192]{0,1:T(8,128)(2,1)S(1)}, bf16[1024,8192]{0,1:T(8,128)(2,1)}, u32[]{:S(2)}) copy-start(bf16[1024,8192]{0,1:T(8,128)(2,1)} %fusion) | copy-start | bytes 50331652 | tf_op jit(solution)/shard_map/cond
  254.5 0.6 copy-start.4
  254.5 0.8 copy-start.3
  255.1 530.7 %reduce-scatter.5.cloned.1.call-start = ((), (), s32[]{:S(2)}) async-start(), calls=%async_computation.4 | async-start | bytes 532480 | tf_op jit(solution)/shard_map/reduce_scatter | solution.py:69
  901.5 100.1 %copy-start.6 = (f32[128,16]{0,1:T(8,128)}, f32[128,16]{0,1:T(8,128)S(1)}, u32[]{:S(2)}) copy-start(f32[128,16]{0,1:T(8,128)S(1)} %get-tuple-element.44) | copy-start | bytes 24580
Sparse Core Ops, SparseCore 0:
  11.0 137.2 all-gather.3
  255.3 55.5 reduce-scatter.2
  315.7 470.1 reduce-scatter.4
where the time goes:
time: 1010 us
  waiting for transfers between devices  530 us (52%)
  blocking collectives  402 us (40%)
  matrix products  49.2 us (5%)
  between operations  14.5 us (1%)
    reduce_scatter x1, waiting for transfers between devices, body(): lax.psum_scatter(col_total, 'own', scatter_dimension=0, tiled=True)  475 us
    psum x1, blocking collectives, body(): curvature, norm_old = lax.psum((curve_local, norm_local), ('own', 'pair'))  113 us
    psum x1, blocking collectives, body(): lax.psum(jnp.sum(new_residual * new_residual, axis=0), ('own', 'pair'))  99.4 us
    all_gather x1, blocking collectives, body(): col_dir = lax.all_gather(dir_low, 'own', axis=0, tiled=True)  73.4 us
    all_gather x1, blocking collectives, body(): col_task = lax.all_gather(task_vals, 'own', axis=0, tiled=True)  67.6 us
    reduce_scatter x1, waiting for transfers between devices, body(): lax.psum_scatter(row_total, 'pair', scatter_dimension=0, tiled=True)  54.9 us
    all_gather x1, blocking collectives, body(): lax.all_gather(dir_low, 'pair', axis=0, tiled=True)  20.8 us
  transfers between devices with their start and end apart: 3, of which 2 were waited for; matrix products, arithmetic and copies ran while one was open for 0% of the time, Pallas kernels for 0%

commit v1 on v0

v1 whole, which is shorter than its diff:
```python
import math

import jax
import jax.numpy as jnp
from jax import lax
from jax.experimental import pallas as pl
from jax.experimental.pallas import tpu as pltpu
from jax.sharding import Mesh
from jax.sharding import PartitionSpec as P

noise_var = 1.0
log2e = math.log2(math.e)
f32, bf16 = jnp.float32, jnp.bfloat16

FEATS, PROBES, LEVELS, LANES = 64, 16, 8, 128
TASK_AT, DIR_AT = FEATS, FEATS + 8
ROW_ROWS, COL_ROWS = DIR_AT, DIR_AT + PROBES
TAIL = 16
DEPTH = 3 * FEATS + TAIL
TILE = 512

SHAPE = (16, 4, 4, 2)
AXES = ("z", "x", "y", "core")
LINE, PLANE = "z", ("x", "y", "core")


def split3(value):
    high = value.astype(bf16)
    rest = value - high.astype(f32)
    mid = rest.astype(bf16)
    return high, mid, (rest - mid.astype(f32)).astype(bf16)


def tail_rows(norm, first):
    high, mid, low = split3(norm)
    row = lax.broadcasted_iota(jnp.int32, (TAIL, norm.shape[1]), 0)
    value = jnp.where(row == first, high.astype(f32), 0.0)
    value = jnp.where(row == first + 1, mid.astype(f32), value)
    value = jnp.where(row == first + 2, low.astype(f32), value)
    ones_at = 3 - first
    return jnp.where((row >= ones_at) & (row < ones_at + 3), 1.0, value).astype(bf16)


def pack_kernel(points_ref, scale_ref, tasks_ref, dir_ref, rows_ref, cols_ref):
    scaled = (points_ref[...].astype(f32) * scale_ref[...]).astype(bf16)
    turned = scaled.astype(f32).T
    task = jnp.broadcast_to(tasks_ref[...].astype(f32), (8, LANES))
    shared = jnp.concatenate([turned, task], axis=0).astype(bf16)
    whole = jnp.concatenate([turned, task, dir_ref[...]], axis=0).astype(bf16)
    for k in range(rows_ref.shape[0]):
        rows_ref[k] = shared
    for k in range(cols_ref.shape[0]):
        cols_ref[k] = whole


def block_kernel(rows_ref, cols_ref, cov_ref, out_ref, row_mat, col_mat, dir_mat):
    n_rows, n_cols = rows_ref.shape[0], cols_ref.shape[0]
    for k in range(n_rows):
        at = pl.ds(k * LANES, LANES)
        scaled = rows_ref[k, :FEATS, :]
        wide = scaled.astype(f32)
        norm = jnp.sum(wide * wide, axis=0, keepdims=True) * (-0.5 * log2e)
        for part in range(3):
            row_mat[part * FEATS : (part + 1) * FEATS, at] = scaled
        row_mat[3 * FEATS :, at] = tail_rows(norm, 3)
    for k in range(n_cols):
        at = pl.ds(k * LANES, LANES)
        wide = cols_ref[k, :FEATS, :].astype(f32)
        norm = jnp.sum(wide * wide, axis=0, keepdims=True) * (-0.5 * log2e)
        high, mid, low = split3(wide * log2e)
        stack = jnp.concatenate([high, mid, low, tail_rows(norm, 0)], axis=0)
        col_mat[at, :] = stack.astype(f32).T.astype(bf16)
        task = cols_ref[k, TASK_AT:DIR_AT, :][0:1].astype(f32)
        dirs = cols_ref[k, DIR_AT:, :].astype(f32)
        dir_mat[:, at] = jnp.concatenate(
            [jnp.where(task == float(level), dirs, 0.0) for level in range(LEVELS)], axis=0
        ).astype(bf16)

    def step(tile, carry):
        base = pl.multiple_of(tile * TILE, TILE)
        exponent = jnp.dot(
            col_mat[...], row_mat[:, pl.ds(base, TILE)], preferred_element_type=f32
        )
        kernel = jnp.exp2(exponent).astype(bf16)
        sums = jnp.dot(dir_mat[...], kernel, preferred_element_type=f32)
        for j in range(TILE // LANES):
            k = tile * (TILE // LANES) + j
            task = rows_ref[k, TASK_AT:DIR_AT, :][0:1].astype(f32)
            cov = jnp.zeros((LEVELS, LANES), f32)
            for level in range(LEVELS):
                cov = cov + jnp.where(task == float(level), cov_ref[:, level : level + 1], 0.0)
            total = jnp.zeros((PROBES, LANES), f32)
            for level in range(LEVELS):
                part = sums[level * PROBES : (level + 1) * PROBES, j * LANES : (j + 1) * LANES]
                total = total + cov[level : level + 1, :] * part
            out_ref[k] = total
        return carry

    lax.fori_loop(0, n_rows * LANES // TILE, step, 0)


def product_kernel(parts_ref, dir_ref, res_ref, product_ref, stats_ref):
    direction, residual = dir_ref[...], res_ref[...]
    product = jnp.sum(parts_ref[...], axis=0) + noise_var * direction
    product_ref[...] = product
    terms = jnp.concatenate(
        [direction * product, residual * residual, residual * product, product * product], axis=0
    )
    sums = jnp.sum(terms.T, axis=0, keepdims=True)
    row = jnp.concatenate([sums, jnp.zeros((1, LANES - sums.shape[1]), f32)], axis=1)
    stats_ref[...] = jnp.broadcast_to(row[None], stats_ref.shape)


def call(kernel, out_shape, n_in, scratch=(), limit=16):
    vmem = pl.BlockSpec(memory_space=pltpu.VMEM)
    many = isinstance(out_shape, (list, tuple))
    return pl.pallas_call(
        kernel,
        out_shape=out_shape,
        in_specs=[vmem] * n_in,
        out_specs=[vmem] * len(out_shape) if many else vmem,
        scratch_shapes=scratch,
        compiler_params=pltpu.CompilerParams(vmem_limit_bytes=limit * 2**20),
    )


def body(points, inv_scale, tasks, task_cov, solution, residual, direction):
    line, plane = SHAPE[0], math.prod(SHAPE[1:])
    dir_t, res_t, sol_t = direction.T, residual.T, solution.T
    row_send, col_send = call(
        pack_kernel,
        [
            jax.ShapeDtypeStruct((plane, ROW_ROWS, LANES), bf16),
            jax.ShapeDtypeStruct((line, COL_ROWS, LANES), bf16),
        ],
        4,
    )(points, inv_scale[None, :], tasks[None, :], dir_t)
    cols = lax.all_to_all(col_send, LINE, 0, 0)
    rows = lax.all_to_all(row_send, PLANE, 0, 0)
    partial = call(
        block_kernel,
        jax.ShapeDtypeStruct((plane, PROBES, LANES), f32),
        3,
        [
            pltpu.VMEM((DEPTH, plane * LANES), bf16),
            pltpu.VMEM((line * LANES, DEPTH), bf16),
            pltpu.VMEM((LEVELS * PROBES, line * LANES), bf16),
        ],
        limit=40,
    )(rows, cols, task_cov)
    parts = lax.all_to_all(partial, PLANE, 0, 0)
    product, stats = call(
        product_kernel,
        [
            jax.ShapeDtypeStruct((PROBES, LANES), f32),
            jax.ShapeDtypeStruct((plane, 1, LANES), f32),
        ],
        3,
    )(parts, dir_t, res_t)
    stats = jnp.sum(lax.all_to_all(stats, PLANE, 0, 0), axis=0)
    stats = jnp.broadcast_to(stats[None], (line,) + stats.shape)
    stats = jnp.sum(lax.all_to_all(stats, LINE, 0, 0), axis=(0, 1))
    curvature, norm_old, cross, norm_product = (
        stats[k * PROBES : (k + 1) * PROBES][:, None] for k in range(4)
    )
    step_size = norm_old / curvature
    norm_new = norm_old + step_size * (step_size * norm_product - 2.0 * cross)
    new_residual = res_t - step_size * product
    new_solution = sol_t + step_size * dir_t
    new_direction = new_residual + norm_new / norm_old * dir_t
    return (new_solution.T, new_residual.T, new_direction.T)


def solution(mesh):
    fine = Mesh(mesh.devices.reshape(SHAPE), AXES)
    rows, flat = P(AXES, None), P(AXES)
    return jax.shard_map(
        body,
        mesh=fine,
        in_specs=(rows, P(), flat, P(), rows, rows, rows),
        out_specs=(rows, rows, rows),
        check_vma=False,
    )
```

time: 1010 us -> 112 us (0.11)
  waiting for transfers between devices: 530 us -> 0 us
  blocking collectives: 402 us -> 98.2 us
  matrix products: 49.2 us -> 0 us
  between operations: 14.5 us -> 0.7 us
    reduce_scatter x2 -> x0, waiting for transfers between devices: 530 us -> none  [the longest x1 475 us: body(): lax.psum_scatter(col_total, 'own', scatter_dimension=0, tiled=True)]
    psum x2 -> x0, blocking collectives: 213 us -> none  [the longest x1 113 us: body(): curvature, norm_old = lax.psum((curve_local, norm_local), ('own', 'pair'))]
    all_gather x5 -> x0, blocking collectives: 190 us -> none  [the longest x1 73.4 us: body(): col_dir = lax.all_gather(dir_low, 'own', axis=0, tiled=True)]
    all_to_all x0 -> x5, blocking collectives: none -> 98.2 us  [the longest x1 32.6 us: body(): cols = lax.all_to_all(col_send, LINE, 0, 0)]
    dot_general x5 -> x0, matrix products: 49.2 us -> none  [the longest x1 18.7 us: kernel_tile(): lax.dot_general(row_scaled, col_scaled, (((1,), (1,)), ((), ())), preferr...]
  transfers between devices with their start and end apart: 3 -> 0, of which waited for: 2 -> 0; matrix products, arithmetic and copies ran while one was open for 0% -> 0% of each run, Pallas kernels for 0% -> 0%
where the time goes in v1:
time: 112 us
  blocking collectives  98.2 us (88%)
  Pallas kernels  9.15 us (8%)
  local copies, waits for them, and re-layouts  2.11 us (2%)
  other arithmetic  1.49 us (1%)
    all_to_all x1, blocking collectives, body(): cols = lax.all_to_all(col_send, LINE, 0, 0)  32.6 us
    all_to_all x1, blocking collectives, body(): rows = lax.all_to_all(row_send, PLANE, 0, 0)  21.9 us
    all_to_all x1, blocking collectives, body(): parts = lax.all_to_all(partial, PLANE, 0, 0)  17.1 us
    all_to_all x1, blocking collectives, body(): stats = jnp.sum(lax.all_to_all(stats, LINE, 0, 0), axis=(0, 1))  16.2 us
    all_to_all x1, blocking collectives, body(): stats = jnp.sum(lax.all_to_all(stats, PLANE, 0, 0), axis=0)  10.4 us
    pallas_call x1, Pallas kernels, body(): call(block_kernel, jax.ShapeDtypeStruct((plane, PROBES, LANES), f32), 3,...  8.88 us

profile of v1, /device:TPU:1, one launch (start us, length us, event | category | flops | bytes accessed | tf_op | source)
XLA Modules:
  0.0 111.7 jit_solution(279910235519811161)
XLA Ops:
  0.6 0.0 copy-start
  0.6 0.8 copy.12.points_ref
  1.5 0.0 copy-start.3
  1.5 0.0 copy-start.4
  1.5 0.0 copy-done
  1.5 0.6 copy-done.3
  2.1 0.0 copy-done.4
  2.2 0.1 shard_map.94
  2.3 21.9 %all_to_all.25.rows_ref = bf16[32,72,128]{2,1,0:T(8,128)(2,1)S(1)} all-to-all(bf16[32,72,128]{2,1,0:T(8,128)(2,1)S(1)} %get-tuple-element.7), channel_id=1, replica_groups=mesh['z'=16,'x'=4,'y'=4,'core'=2] {'x','y','core'}, dimensions={0} | all-to-all | bytes 1179648 | tf_op jit(solution)/shard_map/all_to_all | solution.py:139
  24.2 0.0 copy-start.2
  24.2 32.6 %all_to_all.26.cols_ref = bf16[16,88,128]{2,1,0:T(8,128)(2,1)S(1)} all-to-all(bf16[16,88,128]{2,1,0:T(8,128)(2,1)S(1)} %get-tuple-element.8), channel_id=1, replica_groups=mesh['z'=16,'x'=4,'y'=4,'core'=2] {'z'}, dimensions={0} | all-to-all | bytes 720896 | tf_op jit(solution)/shard_map/all_to_all | solution.py:138
  56.8 0.0 copy-done.2
  56.8 8.9 %shard_map.95 = f32[32,16,128]{2,1,0:T(8,128)S(1)} custom-call(bf16[32,72,128]{2,1,0:T(8,128)(2,1)S(1)} %all_to_all.25.rows_ref, bf16[16,88,128]{2,1,0:T(8,128)(2,1)S(1)} %all_to_all.26.cols_ref, f32[8,8]{1,0:T(8,128)S(1)} %copy-done.2), custom_call_target="tpu_custom_call" | custom-call | tf_op jit(solution)/shard_map/pallas_call | solution.py:140
  65.7 0.0 copy-start.1
  65.7 17.1 %all_to_all.27.parts_ref = f32[32,16,128]{2,1,0:T(8,128)S(1)} all-to-all(f32[32,16,128]{2,1,0:T(8,128)S(1)} %shard_map.95), channel_id=1, replica_groups=mesh['z'=16,'x'=4,'y'=4,'core'=2] {'x','y','core'}, dimensions={0} | all-to-all | bytes 524288 | tf_op jit(solution)/shard_map/all_to_all | solution.py:151
  82.8 0.0 copy-done.1
  82.8 0.1 shard_map.96
  83.0 10.4 %all_to_all.28 = f32[32,1,128]{2,1,0:T(1,128)S(1)} all-to-all(f32[32,1,128]{2,1,0:T(1,128)S(1)} %get-tuple-element.9), channel_id=1, replica_groups=mesh['z'=16,'x'=4,'y'=4,'core'=2] {'x','y','core'}, dimensions={0} | all-to-all | bytes 32768 | tf_op jit(solution)/shard_map/all_to_all | solution.py:160
  93.4 0.1 reduce_sum.18
  93.5 16.2 %all_to_all.29 = f32[16,1,128]{2,1,0:T(1,128)S(1)} all-to-all(f32[16,1,128]{2,1,0:T(1,128)S(1)} %broadcast_in_dim.8), channel_id=1, replica_groups=mesh['z'=16,'x'=4,'y'=4,'core'=2] {'z'}, dimensions={0} | all-to-all | bytes 16384 | tf_op jit(solution)/shard_map/all_to_all | solution.py:162
  109.7 0.1 add_divide_fusion
  109.7 0.6 copy-done.5
  110.3 0.7 multiply_add_fusion
  111.0 0.7 add_bitcast_fusion
  (3 shorter events, 0.0 us)
Async XLA Ops:
  0.6 0.9 copy-start
  1.5 0.7 copy-start.3
  1.5 0.7 copy-start.4
  24.2 32.6 %copy-start.2 = (f32[8,8]{1,0:T(8,128)S(1)}, f32[8,8]{1,0:T(8,128)}, u32[]{:S(2)}) copy-start(f32[8,8]{1,0:T(8,128)} %cov_ref.1) | copy-start | bytes 772
  65.7 17.1 %copy-start.1 = (f32[128,16]{0,1:T(8,128)S(1)}, f32[128,16]{0,1:T(8,128)}, u32[]{:S(2)}) copy-start(f32[128,16]{0,1:T(8,128)} %param.12) | copy-start | bytes 24580
  109.6 0.7 copy-start.5

commit v2 on v1

--- a/solution.py
+++ b/solution.py
@@ -9,15 +9,14 @@
 from jax.sharding import PartitionSpec as P
 
 noise_var = 1.0
-log2e = math.log2(math.e)
 f32, bf16 = jnp.float32, jnp.bfloat16
 
 FEATS, PROBES, LEVELS, LANES = 64, 16, 8, 128
 TASK_AT, DIR_AT = FEATS, FEATS + 8
 ROW_ROWS, COL_ROWS = DIR_AT, DIR_AT + PROBES
 TAIL = 16
-DEPTH = 3 * FEATS + TAIL
-TILE = 512
+DEPTH = FEATS + TAIL
+TILE = 1024
 
 SHAPE = (16, 4, 4, 2)
 AXES = ("z", "x", "y", "core")
@@ -42,13 +41,11 @@
 
 
 def pack_kernel(points_ref, scale_ref, tasks_ref, dir_ref, rows_ref, cols_ref):
-    scaled = (points_ref[...].astype(f32) * scale_ref[...]).astype(bf16)
-    turned = scaled.astype(f32).T
+    scale = jnp.broadcast_to(scale_ref[...], (LANES, FEATS)).T
+    scaled = points_ref[...].astype(f32) * scale
     task = jnp.broadcast_to(tasks_ref[...].astype(f32), (8, LANES))
-    shared = jnp.concatenate([turned, task], axis=0).astype(bf16)
-    whole = jnp.concatenate([turned, task, dir_ref[...]], axis=0).astype(bf16)
-    for k in range(rows_ref.shape[0]):
-        rows_ref[k] = shared
+    rows_ref[...] = jnp.concatenate([scaled, task], axis=0).astype(bf16)
+    whole = jnp.concatenate([scaled, task, dir_ref[...]], axis=0).astype(bf16)
     for k in range(cols_ref.shape[0]):
         cols_ref[k] = whole
 
@@ -59,16 +56,15 @@
         at = pl.ds(k * LANES, LANES)
         scaled = rows_ref[k, :FEATS, :]
         wide = scaled.astype(f32)
-        norm = jnp.sum(wide * wide, axis=0, keepdims=True) * (-0.5 * log2e)
-        for part in range(3):
-            row_mat[part * FEATS : (part + 1) * FEATS, at] = scaled
-        row_mat[3 * FEATS :, at] = tail_rows(norm, 3)
+        norm = jnp.sum(wide * wide, axis=0, keepdims=True) * -0.5
+        row_mat[:FEATS, at] = scaled
+        row_mat[FEATS:, at] = tail_rows(norm, 3)
     for k in range(n_cols):
         at = pl.ds(k * LANES, LANES)
-        wide = cols_ref[k, :FEATS, :].astype(f32)
-        norm = jnp.sum(wide * wide, axis=0, keepdims=True) * (-0.5 * log2e)
-        high, mid, low = split3(wide * log2e)
-        stack = jnp.concatenate([high, mid, low, tail_rows(norm, 0)], axis=0)
+        scaled = cols_ref[k, :FEATS, :]
+        wide = scaled.astype(f32)
+        norm = jnp.sum(wide * wide, axis=0, keepdims=True) * -0.5
+        stack = jnp.concatenate([scaled, tail_rows(norm, 0)], axis=0)
         col_mat[at, :] = stack.astype(f32).T.astype(bf16)
         task = cols_ref[k, TASK_AT:DIR_AT, :][0:1].astype(f32)
         dirs = cols_ref[k, DIR_AT:, :].astype(f32)
@@ -81,7 +77,7 @@
         exponent = jnp.dot(
             col_mat[...], row_mat[:, pl.ds(base, TILE)], preferred_element_type=f32
         )
-        kernel = jnp.exp2(exponent).astype(bf16)
+        kernel = jnp.exp(exponent).astype(bf16)
         sums = jnp.dot(dir_mat[...], kernel, preferred_element_type=f32)
         for j in range(TILE // LANES):
             k = tile * (TILE // LANES) + j
@@ -111,6 +107,20 @@
     stats_ref[...] = jnp.broadcast_to(row[None], stats_ref.shape)
 
 
+def update_kernel(stats_ref, product_ref, dir_ref, res_ref, sol_ref, new_sol_ref, new_res_ref, new_dir_ref):
+    sums = jnp.broadcast_to(jnp.sum(stats_ref[...], axis=0), (LANES, LANES)).T
+    curvature, norm_old, cross, norm_product = (
+        sums[k * PROBES : (k + 1) * PROBES] for k in range(4)
+    )
+    step_size = norm_old / curvature
+    norm_new = norm_old + step_size * (step_size * norm_product - 2.0 * cross)
+    direction = dir_ref[...]
+    new_residual = res_ref[...] - step_size * product_ref[...]
+    new_sol_ref[...] = sol_ref[...] + step_size * direction
+    new_res_ref[...] = new_residual
+    new_dir_ref[...] = new_residual + norm_new / norm_old * direction
+
+
 def call(kernel, out_shape, n_in, scratch=(), limit=16):
     vmem = pl.BlockSpec(memory_space=pltpu.VMEM)
     many = isinstance(out_shape, (list, tuple))
@@ -130,13 +140,13 @@
     row_send, col_send = call(
         pack_kernel,
         [
-            jax.ShapeDtypeStruct((plane, ROW_ROWS, LANES), bf16),
+            jax.ShapeDtypeStruct((ROW_ROWS, LANES), bf16),
             jax.ShapeDtypeStruct((line, COL_ROWS, LANES), bf16),
         ],
         4,
-    )(points, inv_scale[None, :], tasks[None, :], dir_t)
+    )(points.T, inv_scale[None, :], tasks[None, :], dir_t)
     cols = lax.all_to_all(col_send, LINE, 0, 0)
-    rows = lax.all_to_all(row_send, PLANE, 0, 0)
+    rows = lax.all_gather(row_send, PLANE)
     partial = call(
         block_kernel,
         jax.ShapeDtypeStruct((plane, PROBES, LANES), f32),
@@ -159,15 +169,11 @@
     )(parts, dir_t, res_t)
     stats = jnp.sum(lax.all_to_all(stats, PLANE, 0, 0), axis=0)
     stats = jnp.broadcast_to(stats[None], (line,) + stats.shape)
-    stats = jnp.sum(lax.all_to_all(stats, LINE, 0, 0), axis=(0, 1))
-    curvature, norm_old, cross, norm_product = (
-        stats[k * PROBES : (k + 1) * PROBES][:, None] for k in range(4)
+    stats = lax.all_to_all(stats, LINE, 0, 0)
+    like = jax.ShapeDtypeStruct((PROBES, LANES), f32)
+    new_solution, new_residual, new_direction = call(update_kernel, [like] * 3, 5)(
+        stats, product, dir_t, res_t, sol_t
     )
-    step_size = norm_old / curvature
-    norm_new = norm_old + step_size * (step_size * norm_product - 2.0 * cross)
-    new_residual = res_t - step_size * product
-    new_solution = sol_t + step_size * dir_t
-    new_direction = new_residual + norm_new / norm_old * dir_t
     return (new_solution.T, new_residual.T, new_direction.T)
 
 

time: 112 us -> 102 us (0.911)
  blocking collectives: 98.2 us -> 73.1 us
  starting transfers between devices: 0 us -> 15.7 us
  other arithmetic: 1.49 us -> 0.05 us
    all_to_all x3 -> x1, blocking collectives: 70.7 us -> 22.8 us  [body(): stats = lax.all_to_all(stats, LINE, 0, 0)]
    all_gather x0 -> x1, blocking collectives: none -> 25.9 us  [body(): rows = lax.all_gather(row_send, PLANE)]
    all_to_all x0 -> x1, starting transfers between devices: none -> 15.7 us  [body(): cols = lax.all_to_all(col_send, LINE, 0, 0)]
    all_to_all x1, blocking collectives: 17.1 us -> 13.9 us  [body(): parts = lax.all_to_all(partial, PLANE, 0, 0)]
    pallas_call x1 -> x2, Pallas kernels: 0.13 us -> 1.53 us  [the longest x1 0.82 us: body(): call(pack_kernel, [jax.ShapeDtypeStruct((ROW_ROWS, LANES), bf16), jax.Sha...]
  transfers between devices with their start and end apart: 0 -> 1, of which waited for: 0 -> 0; matrix products, arithmetic and copies ran while one was open for 0% -> 0% of each run, Pallas kernels for 0% -> 0%
where the time goes in v2:
time: 102 us; the launch traced here: 101 us
  blocking collectives  73.1 us (72%)
  starting transfers between devices  15.7 us (15%)
  Pallas kernels  9.44 us (9%)
  local copies, waits for them, and re-layouts  2.1 us (2%)
    all_gather x1, blocking collectives, body(): rows = lax.all_gather(row_send, PLANE)  25.9 us
    all_to_all x1, blocking collectives, body(): stats = lax.all_to_all(stats, LINE, 0, 0)  22.8 us
    all_to_all x1, starting transfers between devices, body(): cols = lax.all_to_all(col_send, LINE, 0, 0)  15.7 us
    all_to_all x1, blocking collectives, body(): parts = lax.all_to_all(partial, PLANE, 0, 0)  13.9 us
    all_to_all x1, blocking collectives, body(): stats = jnp.sum(lax.all_to_all(stats, PLANE, 0, 0), axis=0)  10.4 us
    pallas_call x1, Pallas kernels, body(): call(block_kernel, jax.ShapeDtypeStruct((plane, PROBES, LANES), f32), 3,...  7.77 us
    unnamed x16, local copies, waits for them, and re-layouts  2.09 us
  transfers between devices with their start and end apart: 1, of which 0 were waited for; matrix products, arithmetic and copies ran while one was open for 0% of the time, Pallas kernels for 0%

profile of v2, /device:TPU:1, one launch (start us, length us, event | category | flops | bytes accessed | tf_op | source)
XLA Modules:
  0.0 101.1 jit_solution(11131652801355670730)
XLA Ops:
  0.6 0.0 copy-start.6
  0.6 0.0 copy-start.7
  0.7 0.6 copy-done.6
  1.3 0.0 copy-done.7
  1.3 0.7 copy-done
  2.0 0.7 copy-done.3
  2.7 0.8 shard_map.94
  3.5 15.7 %all-to-all-start = ((bf16[16,88,128]{2,1,0:T(8,128)(2,1)}), bf16[16,88,128]{2,1,0:T(8,128)(2,1)S(1)}, u32[]{:S(2)}, u32[]{:S(2)}) async-start(bf16[16,88,128]{2,1,0:T(8,128)(2,1)} %get-tuple-element.11), calls=%async_computation | async-start | bytes 720896 | tf_op jit(solution)/shard_map/all_to_all | solution.py:148
  19.3 0.0 copy-start.5
  19.3 25.9 %all-gather = bf16[2304,128]{1,0:T(8,128)(2,1)S(1)} all-gather(bf16[72,128]{1,0:T(8,128)(2,1)S(1)} %get-tuple-element.10), channel_id=2, replica_groups=mesh['z'=16,'x'=4,'y'=4,'core'=2] {'x','y','core'}, dimensions={0}, use_global_device_ids=true | all-gather | bytes 608256 | tf_op jit(solution)/shard_map/all_gather | solution.py:149
  45.2 0.0 all-to-all-done.cols_ref
  45.2 0.0 copy-done.5
  45.2 7.8 %shard_map.95 = f32[32,16,128]{2,1,0:T(8,128)S(1)} custom-call(bf16[32,72,128]{2,1,0:T(8,128)(2,1)S(1)} %bitcast.10, bf16[16,88,128]{2,1,0:T(8,128)(2,1)S(1)} %all-to-all-done.cols_ref, f32[8,8]{1,0:T(8,128)S(1)} %copy-done.5), custom_call_target="tpu_custom_call" | custom-call | tf_op jit(solution)/shard_map/pallas_call | solution.py:150
  53.0 0.0 copy-start.1
  53.0 0.0 copy-start.2
  53.0 13.9 %all_to_all.20.parts_ref = f32[32,16,128]{2,1,0:T(8,128)S(1)} all-to-all(f32[32,16,128]{2,1,0:T(8,128)S(1)} %shard_map.95), channel_id=1, replica_groups=mesh['z'=16,'x'=4,'y'=4,'core'=2] {'x','y','core'}, dimensions={0} | all-to-all | bytes 524288 | tf_op jit(solution)/shard_map/all_to_all | solution.py:161
  66.9 0.0 copy-done.1
  67.0 0.0 copy-done.2
  67.0 0.1 shard_map.96
  67.1 10.4 %all_to_all.21 = f32[32,1,128]{2,1,0:T(1,128)S(1)} all-to-all(f32[32,1,128]{2,1,0:T(1,128)S(1)} %get-tuple-element.12), channel_id=1, replica_groups=mesh['z'=16,'x'=4,'y'=4,'core'=2] {'x','y','core'}, dimensions={0} | all-to-all | bytes 32768 | tf_op jit(solution)/shard_map/all_to_all | solution.py:170
  77.5 0.1 reduce_sum.9
  77.6 22.8 %all_to_all.22.stats_ref = f32[16,1,128]{2,1,0:T(1,128)S(1)} all-to-all(f32[16,1,128]{2,1,0:T(1,128)S(1)} %broadcast_in_dim.14), channel_id=1, replica_groups=mesh['z'=16,'x'=4,'y'=4,'core'=2] {'z'}, dimensions={0} | all-to-all | bytes 16384 | tf_op jit(solution)/shard_map/all_to_all | solution.py:172
  100.4 0.0 copy-done.4
  100.4 0.7 shard_map.97
  (4 shorter events, 0.0 us)
Async XLA Ops:
  0.6 0.7 copy-start.6
  0.6 0.7 copy-start.7
  1.3 0.7 copy-start
  2.0 0.7 copy-start.3
  3.5 41.7 %all-to-all-start = ((bf16[16,88,128]{2,1,0:T(8,128)(2,1)}), bf16[16,88,128]{2,1,0:T(8,128)(2,1)S(1)}, u32[]{:S(2)}, u32[]{:S(2)}) async-start(bf16[16,88,128]{2,1,0:T(8,128)(2,1)} %get-tuple-element.11), calls=%async_computation | async-start | bytes 720896 | tf_op jit(solution)/shard_map/all_to_all | solution.py:148
  19.3 26.0 %copy-start.5 = (f32[8,8]{1,0:T(8,128)S(1)}, f32[8,8]{1,0:T(8,128)}, u32[]{:S(2)}) copy-start(f32[8,8]{1,0:T(8,128)} %cov_ref.1) | copy-start | bytes 772
  53.0 13.9 %copy-start.1 = (f32[128,16]{0,1:T(8,128)S(1)}, f32[128,16]{0,1:T(8,128)}, u32[]{:S(2)}) copy-start(f32[128,16]{0,1:T(8,128)} %param.13) | copy-start | bytes 24580
  53.0 13.9 %copy-start.2 = (f32[128,16]{0,1:T(8,128)S(1)}, f32[128,16]{0,1:T(8,128)}, u32[]{:S(2)}) copy-start(f32[128,16]{0,1:T(8,128)} %param.12) | copy-start | bytes 24580
  77.6 22.8 %copy-start.4 = (f32[128,16]{0,1:T(8,128)S(1)}, f32[128,16]{0,1:T(8,128)}, u32[]{:S(2)}) copy-start(f32[128,16]{0,1:T(8,128)} %param.11) | copy-start | bytes 24580

commit v3 on v2

--- a/solution.py
+++ b/solution.py
@@ -169,7 +169,7 @@
     )(parts, dir_t, res_t)
     stats = jnp.sum(lax.all_to_all(stats, PLANE, 0, 0), axis=0)
     stats = jnp.broadcast_to(stats[None], (line,) + stats.shape)
-    stats = lax.all_to_all(stats, LINE, 0, 0)
+    stats = lax.all_to_all(stats, LINE, 0, 0, axis_index_groups=[[(k + 8) % 16 for k in range(16)]])
     like = jax.ShapeDtypeStruct((PROBES, LANES), f32)
     new_solution, new_residual, new_direction = call(update_kernel, [like] * 3, 5)(
         stats, product, dir_t, res_t, sol_t

time: 102 us -> 93.2 us (0.914)
  blocking collectives: 73.1 us -> 64.6 us
    all_to_all x1, blocking collectives: 22.8 us -> 14.4 us  [body(): lax.all_to_all(stats, LINE, 0, 0, axis_index_groups=[[(k + 8) % 16 for k...]
where the time goes in v3:
time: 93.2 us; the launch traced here: 92.7 us
  blocking collectives  64.6 us (69%)
  starting transfers between devices  15.7 us (17%)
  Pallas kernels  9.44 us (10%)
  local copies, waits for them, and re-layouts  2.1 us (2%)
    all_gather x1, blocking collectives, body(): rows = lax.all_gather(row_send, PLANE)  25.9 us
    all_to_all x1, starting transfers between devices, body(): cols = lax.all_to_all(col_send, LINE, 0, 0)  15.7 us
    all_to_all x1, blocking collectives, body(): lax.all_to_all(stats, LINE, 0, 0, axis_index_groups=[[(k + 8) % 16 for k...  14.4 us
    all_to_all x1, blocking collectives, body(): parts = lax.all_to_all(partial, PLANE, 0, 0)  13.9 us
    all_to_all x1, blocking collectives, body(): stats = jnp.sum(lax.all_to_all(stats, PLANE, 0, 0), axis=0)  10.4 us
    pallas_call x1, Pallas kernels, body(): call(block_kernel, jax.ShapeDtypeStruct((plane, PROBES, LANES), f32), 3,...  7.77 us
    unnamed x16, local copies, waits for them, and re-layouts  2.09 us
  transfers between devices with their start and end apart: 1, of which 0 were waited for; matrix products, arithmetic and copies ran while one was open for 0% of the time, Pallas kernels for 0%

profile of v3, /device:TPU:1, one launch (start us, length us, event | category | flops | bytes accessed | tf_op | source)
XLA Modules:
  0.0 92.7 jit_solution(4336541155009100208)
XLA Ops:
  0.6 0.0 copy-start.6
  0.6 0.0 copy-start.7
  0.7 0.6 copy-done.6
  1.3 0.0 copy-done.7
  1.3 0.7 copy-done
  2.0 0.7 copy-done.3
  2.7 0.8 shard_map.94
  3.5 15.7 %all-to-all-start = ((bf16[16,88,128]{2,1,0:T(8,128)(2,1)}), bf16[16,88,128]{2,1,0:T(8,128)(2,1)S(1)}, u32[]{:S(2)}, u32[]{:S(2)}) async-start(bf16[16,88,128]{2,1,0:T(8,128)(2,1)} %get-tuple-element.11), calls=%async_computation | async-start | bytes 720896 | tf_op jit(solution)/shard_map/all_to_all | solution.py:148
  19.3 0.0 copy-start.5
  19.3 25.9 %all-gather = bf16[2304,128]{1,0:T(8,128)(2,1)S(1)} all-gather(bf16[72,128]{1,0:T(8,128)(2,1)S(1)} %get-tuple-element.10), channel_id=2, replica_groups=mesh['z'=16,'x'=4,'y'=4,'core'=2] {'x','y','core'}, dimensions={0}, use_global_device_ids=true | all-gather | bytes 608256 | tf_op jit(solution)/shard_map/all_gather | solution.py:149
  45.2 0.0 all-to-all-done.cols_ref
  45.2 0.0 copy-done.5
  45.2 7.8 %shard_map.95 = f32[32,16,128]{2,1,0:T(8,128)S(1)} custom-call(bf16[32,72,128]{2,1,0:T(8,128)(2,1)S(1)} %bitcast.10, bf16[16,88,128]{2,1,0:T(8,128)(2,1)S(1)} %all-to-all-done.cols_ref, f32[8,8]{1,0:T(8,128)S(1)} %copy-done.5), custom_call_target="tpu_custom_call" | custom-call | tf_op jit(solution)/shard_map/pallas_call | solution.py:150
  53.0 0.0 copy-start.1
  53.0 0.0 copy-start.2
  53.0 13.9 %all_to_all.20.parts_ref = f32[32,16,128]{2,1,0:T(8,128)S(1)} all-to-all(f32[32,16,128]{2,1,0:T(8,128)S(1)} %shard_map.95), channel_id=1, replica_groups=mesh['z'=16,'x'=4,'y'=4,'core'=2] {'x','y','core'}, dimensions={0} | all-to-all | bytes 524288 | tf_op jit(solution)/shard_map/all_to_all | solution.py:161
  66.9 0.0 copy-done.1
  67.0 0.0 copy-done.2
  67.0 0.1 shard_map.96
  67.1 10.4 %all_to_all.21 = f32[32,1,128]{2,1,0:T(1,128)S(1)} all-to-all(f32[32,1,128]{2,1,0:T(1,128)S(1)} %get-tuple-element.12), channel_id=1, replica_groups=mesh['z'=16,'x'=4,'y'=4,'core'=2] {'x','y','core'}, dimensions={0} | all-to-all | bytes 32768 | tf_op jit(solution)/shard_map/all_to_all | solution.py:170
  77.5 0.1 reduce_sum.9
  77.6 14.4 %all_to_all.22.stats_ref = f32[16,1,128]{2,1,0:T(1,128)S(1)} all-to-all(f32[16,1,128]{2,1,0:T(1,128)S(1)} %broadcast_in_dim.14), channel_id=1, replica_groups={{256,288,320,352,384,416,448,480,0,32,64,96,128,160,192,224},{257,289,3..., dimensions={0} | all-to-all | bytes 16384 | tf_op jit(solution)/shard_map/all_to_all | solution.py:172
  92.0 0.0 copy-done.4
  92.0 0.7 shard_map.97
  (4 shorter events, 0.0 us)
Async XLA Ops:
  0.6 0.7 copy-start.6
  0.6 0.7 copy-start.7
  1.3 0.7 copy-start
  2.0 0.7 copy-start.3
  3.5 41.7 %all-to-all-start = ((bf16[16,88,128]{2,1,0:T(8,128)(2,1)}), bf16[16,88,128]{2,1,0:T(8,128)(2,1)S(1)}, u32[]{:S(2)}, u32[]{:S(2)}) async-start(bf16[16,88,128]{2,1,0:T(8,128)(2,1)} %get-tuple-element.11), calls=%async_computation | async-start | bytes 720896 | tf_op jit(solution)/shard_map/all_to_all | solution.py:148
  19.3 26.0 %copy-start.5 = (f32[8,8]{1,0:T(8,128)S(1)}, f32[8,8]{1,0:T(8,128)}, u32[]{:S(2)}) copy-start(f32[8,8]{1,0:T(8,128)} %cov_ref.1) | copy-start | bytes 772
  53.0 13.9 %copy-start.1 = (f32[128,16]{0,1:T(8,128)S(1)}, f32[128,16]{0,1:T(8,128)}, u32[]{:S(2)}) copy-start(f32[128,16]{0,1:T(8,128)} %param.13) | copy-start | bytes 24580
  53.0 13.9 %copy-start.2 = (f32[128,16]{0,1:T(8,128)S(1)}, f32[128,16]{0,1:T(8,128)}, u32[]{:S(2)}) copy-start(f32[128,16]{0,1:T(8,128)} %param.12) | copy-start | bytes 24580
  77.6 14.4 %copy-start.4 = (f32[128,16]{0,1:T(8,128)S(1)}, f32[128,16]{0,1:T(8,128)}, u32[]{:S(2)}) copy-start(f32[128,16]{0,1:T(8,128)} %param.11) | copy-start | bytes 24580

commit v4 on v3

--- a/solution.py
+++ b/solution.py
@@ -21,6 +21,8 @@
 SHAPE = (16, 4, 4, 2)
 AXES = ("z", "x", "y", "core")
 LINE, PLANE = "z", ("x", "y", "core")
+GATHER_ORDER = [[(k + 12) % SHAPE[0] for k in range(SHAPE[0])]]
+SCALAR_ORDER = [[(k + 8) % SHAPE[0] for k in range(SHAPE[0])]]
 
 
 def split3(value):
@@ -40,12 +42,19 @@
     return jnp.where((row >= ones_at) & (row < ones_at + 3), 1.0, value).astype(bf16)
 
 
-def pack_kernel(points_ref, scale_ref, tasks_ref, dir_ref, rows_ref, cols_ref):
+def pack_kernel(points_in, scale_in, tasks_in, dir_in, rows_ref, cols_ref, points_ref, scale_ref, tasks_ref, dir_ref, sems):
+    pairs = ((points_in, points_ref), (scale_in, scale_ref), (tasks_in, tasks_ref), (dir_in, dir_ref))
+    copies = [pltpu.make_async_copy(src, dst, sems.at[k]) for k, (src, dst) in enumerate(pairs)]
+    for copy in copies:
+        copy.start()
+    for copy in copies:
+        copy.wait()
     scale = jnp.broadcast_to(scale_ref[...], (LANES, FEATS)).T
     scaled = points_ref[...].astype(f32) * scale
     task = jnp.broadcast_to(tasks_ref[...].astype(f32), (8, LANES))
-    rows_ref[...] = jnp.concatenate([scaled, task], axis=0).astype(bf16)
+    shared = jnp.concatenate([scaled, task], axis=0).astype(bf16)
     whole = jnp.concatenate([scaled, task, dir_ref[...]], axis=0).astype(bf16)
+    rows_ref[...] = shared
     for k in range(cols_ref.shape[0]):
         cols_ref[k] = whole
 
@@ -121,13 +130,13 @@
     new_dir_ref[...] = new_residual + norm_new / norm_old * direction
 
 
-def call(kernel, out_shape, n_in, scratch=(), limit=16):
+def call(kernel, out_shape, n_in, scratch=(), limit=16, space=pltpu.VMEM):
     vmem = pl.BlockSpec(memory_space=pltpu.VMEM)
     many = isinstance(out_shape, (list, tuple))
     return pl.pallas_call(
         kernel,
         out_shape=out_shape,
-        in_specs=[vmem] * n_in,
+        in_specs=[pl.BlockSpec(memory_space=space)] * n_in,
         out_specs=[vmem] * len(out_shape) if many else vmem,
         scratch_shapes=scratch,
         compiler_params=pltpu.CompilerParams(vmem_limit_bytes=limit * 2**20),
@@ -144,8 +153,17 @@
             jax.ShapeDtypeStruct((line, COL_ROWS, LANES), bf16),
         ],
         4,
+        [
+            pltpu.VMEM((FEATS, LANES), bf16),
+            pltpu.VMEM((1, FEATS), f32),
+            pltpu.VMEM((1, LANES), jnp.int32),
+            pltpu.VMEM((PROBES, LANES), f32),
+            pltpu.SemaphoreType.DMA((4,)),
+        ],
+        limit=60,
+        space=pl.ANY,
     )(points.T, inv_scale[None, :], tasks[None, :], dir_t)
-    cols = lax.all_to_all(col_send, LINE, 0, 0)
+    cols = lax.all_to_all(col_send, LINE, 0, 0, axis_index_groups=GATHER_ORDER)
     rows = lax.all_gather(row_send, PLANE)
     partial = call(
         block_kernel,
@@ -169,7 +187,7 @@
     )(parts, dir_t, res_t)
     stats = jnp.sum(lax.all_to_all(stats, PLANE, 0, 0), axis=0)
     stats = jnp.broadcast_to(stats[None], (line,) + stats.shape)
-    stats = lax.all_to_all(stats, LINE, 0, 0, axis_index_groups=[[(k + 8) % 16 for k in range(16)]])
+    stats = lax.all_to_all(stats, LINE, 0, 0, axis_index_groups=SCALAR_ORDER)
     like = jax.ShapeDtypeStruct((PROBES, LANES), f32)
     new_solution, new_residual, new_direction = call(update_kernel, [like] * 3, 5)(
         stats, product, dir_t, res_t, sol_t

time: 93.2 us -> 91 us (0.976)
  local copies, waits for them, and re-layouts: 2.1 us -> 0.04 us
  blocking collectives: 64.6 us -> 63.4 us
    unnamed x16 -> x10, local copies, waits for them, and re-layouts: 2.09 us -> 0.03 us
    all_to_all x1, blocking collectives: 14.4 us -> 12.8 us  [body(): stats = lax.all_to_all(stats, LINE, 0, 0, axis_index_groups=SCALAR_ORDER)]
where the time goes in v4:
time: 91 us; the launch traced here: 90.3 us
  blocking collectives  63.4 us (70%)
  starting transfers between devices  15.9 us (17%)
  Pallas kernels  10.2 us (11%)
    all_gather x1, blocking collectives, body(): rows = lax.all_gather(row_send, PLANE)  26.2 us
    all_to_all x1, starting transfers between devices, body(): cols = lax.all_to_all(col_send, LINE, 0, 0, axis_index_groups=GATHER_ORDER)  15.9 us
    all_to_all x1, blocking collectives, body(): parts = lax.all_to_all(partial, PLANE, 0, 0)  13.9 us
    all_to_all x1, blocking collectives, body(): stats = lax.all_to_all(stats, LINE, 0, 0, axis_index_groups=SCALAR_ORDER)  12.8 us
    all_to_all x1, blocking collectives, body(): stats = jnp.sum(lax.all_to_all(stats, PLANE, 0, 0), axis=0)  10.4 us
    pallas_call x1, Pallas kernels, body(): call(block_kernel, jax.ShapeDtypeStruct((plane, PROBES, LANES), f32), 3,...  7.76 us
  transfers between devices with their start and end apart: 1, of which 0 were waited for; matrix products, arithmetic and copies ran while one was open for 0% of the time, Pallas kernels for 0%

profile of v4, /device:TPU:1, one launch (start us, length us, event | category | flops | bytes accessed | tf_op | source)
XLA Modules:
  0.0 90.3 jit_solution(8993564751771451412)
XLA Ops:
  0.6 1.6 %shard_map.94 = (bf16[72,128]{1,0:T(8,128)(2,1)}, bf16[16,88,128]{2,1,0:T(8,128)(2,1)}) custom-call(bf16[64,128]{1,0:T(8,128)(2,1)} %bitcast.17, f32[1,64]{1,0:T(1,128)} %bitcast.18, s32[1,128]{1,0:T(1,128)} %bitcast.19, f32[16,128]{1,0:T(8,128)} %bitcast.11), custom_call_target="tpu_custom_call" | custom-call | tf_op jit(solution)/shard_map/pallas_call | solution.py:149
  2.2 0.0 copy-start.4
  2.2 15.9 %all-to-all-start = ((bf16[16,88,128]{2,1,0:T(8,128)(2,1)}), bf16[16,88,128]{2,1,0:T(8,128)(2,1)S(1)}, u32[]{:S(2)}, u32[]{:S(2)}) async-start(bf16[16,88,128]{2,1,0:T(8,128)(2,1)} %get-tuple-element.11), calls=%async_computation | async-start | bytes 720896 | tf_op jit(solution)/shard_map/all_to_all | solution.py:166
  18.2 0.0 copy-done.4
  18.2 0.0 copy-start.3
  18.2 26.2 %all-gather = bf16[2304,128]{1,0:T(8,128)(2,1)S(1)} all-gather(bf16[72,128]{1,0:T(8,128)(2,1)S(1)} %copy-done.4), channel_id=2, replica_groups=mesh['z'=16,'x'=4,'y'=4,'core'=2] {'x','y','core'}, dimensions={0}, use_global_device_ids=true | all-gather | bytes 608256 | tf_op jit(solution)/shard_map/all_gather | solution.py:167
  44.4 0.0 all-to-all-done.cols_ref
  44.4 0.0 copy-done.3
  44.4 7.8 %shard_map.95 = f32[32,16,128]{2,1,0:T(8,128)S(1)} custom-call(bf16[32,72,128]{2,1,0:T(8,128)(2,1)S(1)} %bitcast.10, bf16[16,88,128]{2,1,0:T(8,128)(2,1)S(1)} %all-to-all-done.cols_ref, f32[8,8]{1,0:T(8,128)S(1)} %copy-done.3), custom_call_target="tpu_custom_call" | custom-call | tf_op jit(solution)/shard_map/pallas_call | solution.py:168
  52.2 0.0 copy-start
  52.2 0.0 copy-start.1
  52.2 13.9 %all_to_all.20.parts_ref = f32[32,16,128]{2,1,0:T(8,128)S(1)} all-to-all(f32[32,16,128]{2,1,0:T(8,128)S(1)} %shard_map.95), channel_id=1, replica_groups=mesh['z'=16,'x'=4,'y'=4,'core'=2] {'x','y','core'}, dimensions={0} | all-to-all | bytes 524288 | tf_op jit(solution)/shard_map/all_to_all | solution.py:179
  66.1 0.0 copy-done
  66.1 0.0 copy-done.1
  66.1 0.1 shard_map.96
  66.3 10.4 %all_to_all.21 = f32[32,1,128]{2,1,0:T(1,128)S(1)} all-to-all(f32[32,1,128]{2,1,0:T(1,128)S(1)} %get-tuple-element.12), channel_id=1, replica_groups=mesh['z'=16,'x'=4,'y'=4,'core'=2] {'x','y','core'}, dimensions={0} | all-to-all | bytes 32768 | tf_op jit(solution)/shard_map/all_to_all | solution.py:188
  76.7 0.1 reduce_sum.9
  76.8 0.0 copy-start.2
  76.8 12.8 %all_to_all.22.stats_ref = f32[16,1,128]{2,1,0:T(1,128)S(1)} all-to-all(f32[16,1,128]{2,1,0:T(1,128)S(1)} %broadcast_in_dim.14), channel_id=1, replica_groups={{256,288,320,352,384,416,448,480,0,32,64,96,128,160,192,224},{257,289,3..., dimensions={0} | all-to-all | bytes 16384 | tf_op jit(solution)/shard_map/all_to_all | solution.py:190
  89.6 0.0 copy-done.2
  89.6 0.7 shard_map.97
  (1 shorter events, 0.0 us)
Async XLA Ops:
  2.2 16.0 %copy-start.4 = (bf16[72,128]{1,0:T(8,128)(2,1)S(1)}, bf16[72,128]{1,0:T(8,128)(2,1)}, u32[]{:S(2)}) copy-start(bf16[72,128]{1,0:T(8,128)(2,1)} %get-tuple-element.10) | copy-start | bytes 55300
  2.2 42.2 %all-to-all-start = ((bf16[16,88,128]{2,1,0:T(8,128)(2,1)}), bf16[16,88,128]{2,1,0:T(8,128)(2,1)S(1)}, u32[]{:S(2)}, u32[]{:S(2)}) async-start(bf16[16,88,128]{2,1,0:T(8,128)(2,1)} %get-tuple-element.11), calls=%async_computation | async-start | bytes 720896 | tf_op jit(solution)/shard_map/all_to_all | solution.py:166
  18.2 26.2 %copy-start.3 = (f32[8,8]{1,0:T(8,128)S(1)}, f32[8,8]{1,0:T(8,128)}, u32[]{:S(2)}) copy-start(f32[8,8]{1,0:T(8,128)} %cov_ref.1) | copy-start | bytes 772
  52.2 13.9 %copy-start = (f32[128,16]{0,1:T(8,128)S(1)}, f32[128,16]{0,1:T(8,128)}, u32[]{:S(2)}) copy-start(f32[128,16]{0,1:T(8,128)} %param.13) | copy-start | bytes 24580
  52.2 13.9 %copy-start.1 = (f32[128,16]{0,1:T(8,128)S(1)}, f32[128,16]{0,1:T(8,128)}, u32[]{:S(2)}) copy-start(f32[128,16]{0,1:T(8,128)} %param.12) | copy-start | bytes 24580
  76.8 12.8 %copy-start.2 = (f32[128,16]{0,1:T(8,128)S(1)}, f32[128,16]{0,1:T(8,128)}, u32[]{:S(2)}) copy-start(f32[128,16]{0,1:T(8,128)} %param.11) | copy-start | bytes 24580

commit v5 on v4

--- a/solution.py
+++ b/solution.py
@@ -12,11 +12,8 @@
 f32, bf16 = jnp.float32, jnp.bfloat16
 
 FEATS, PROBES, LEVELS, LANES = 64, 16, 8, 128
-TASK_AT, DIR_AT = FEATS, FEATS + 8
-ROW_ROWS, COL_ROWS = DIR_AT, DIR_AT + PROBES
-TAIL = 16
-DEPTH = FEATS + TAIL
-TILE = 1024
+DEPTH, COL_ROWS = FEATS + 16, FEATS + 8 + PROBES
+ROW_TASK, COL_TASK, DIR_AT = 7, 0, FEATS + 8
 
 SHAPE = (16, 4, 4, 2)
 AXES = ("z", "x", "y", "core")
@@ -32,16 +29,6 @@
     return high, mid, (rest - mid.astype(f32)).astype(bf16)
 
 
-def tail_rows(norm, first):
-    high, mid, low = split3(norm)
-    row = lax.broadcasted_iota(jnp.int32, (TAIL, norm.shape[1]), 0)
-    value = jnp.where(row == first, high.astype(f32), 0.0)
-    value = jnp.where(row == first + 1, mid.astype(f32), value)
-    value = jnp.where(row == first + 2, low.astype(f32), value)
-    ones_at = 3 - first
-    return jnp.where((row >= ones_at) & (row < ones_at + 3), 1.0, value).astype(bf16)
-
-
 def pack_kernel(points_in, scale_in, tasks_in, dir_in, rows_ref, cols_ref, points_ref, scale_ref, tasks_ref, dir_ref, sems):
     pairs = ((points_in, points_ref), (scale_in, scale_ref), (tasks_in, tasks_ref), (dir_in, dir_ref))
     copies = [pltpu.make_async_copy(src, dst, sems.at[k]) for k, (src, dst) in enumerate(pairs)]
@@ -50,11 +37,15 @@
     for copy in copies:
         copy.wait()
     scale = jnp.broadcast_to(scale_ref[...], (LANES, FEATS)).T
-    scaled = points_ref[...].astype(f32) * scale
-    task = jnp.broadcast_to(tasks_ref[...].astype(f32), (8, LANES))
-    shared = jnp.concatenate([scaled, task], axis=0).astype(bf16)
-    whole = jnp.concatenate([scaled, task, dir_ref[...]], axis=0).astype(bf16)
-    rows_ref[...] = shared
+    scaled = (points_ref[...].astype(f32) * scale).astype(bf16)
+    wide = scaled.astype(f32)
+    parts = [p.astype(f32) for p in split3(jnp.sum(wide * wide, axis=0, keepdims=True) * -0.5)]
+    task = tasks_ref[...].astype(f32)
+    zero, one = jnp.zeros_like(task), jnp.ones_like(task)
+    row_tail = jnp.concatenate([zero, one, one, one, *parts, task, jnp.zeros((8, LANES), f32)], axis=0)
+    col_tail = jnp.concatenate([task, *parts, one, one, one, zero, dir_ref[...]], axis=0)
+    rows_ref[...] = jnp.concatenate([scaled, row_tail.astype(bf16)], axis=0)
+    whole = jnp.concatenate([scaled, col_tail.astype(bf16)], axis=0)
     for k in range(cols_ref.shape[0]):
         cols_ref[k] = whole
 
@@ -62,46 +53,27 @@
 def block_kernel(rows_ref, cols_ref, cov_ref, out_ref, row_mat, col_mat, dir_mat):
     n_rows, n_cols = rows_ref.shape[0], cols_ref.shape[0]
     for k in range(n_rows):
-        at = pl.ds(k * LANES, LANES)
-        scaled = rows_ref[k, :FEATS, :]
-        wide = scaled.astype(f32)
-        norm = jnp.sum(wide * wide, axis=0, keepdims=True) * -0.5
-        row_mat[:FEATS, at] = scaled
-        row_mat[FEATS:, at] = tail_rows(norm, 3)
+        row_mat[:, k * LANES : (k + 1) * LANES] = rows_ref[k]
     for k in range(n_cols):
         at = pl.ds(k * LANES, LANES)
-        scaled = cols_ref[k, :FEATS, :]
-        wide = scaled.astype(f32)
-        norm = jnp.sum(wide * wide, axis=0, keepdims=True) * -0.5
-        stack = jnp.concatenate([scaled, tail_rows(norm, 0)], axis=0)
-        col_mat[at, :] = stack.astype(f32).T.astype(bf16)
-        task = cols_ref[k, TASK_AT:DIR_AT, :][0:1].astype(f32)
+        col_mat[at, :] = cols_ref[k, :DEPTH, :].astype(f32).T.astype(bf16)
+        task = cols_ref[k, FEATS:DIR_AT, :].astype(f32)[COL_TASK : COL_TASK + 1]
         dirs = cols_ref[k, DIR_AT:, :].astype(f32)
         dir_mat[:, at] = jnp.concatenate(
             [jnp.where(task == float(level), dirs, 0.0) for level in range(LEVELS)], axis=0
         ).astype(bf16)
-
-    def step(tile, carry):
-        base = pl.multiple_of(tile * TILE, TILE)
-        exponent = jnp.dot(
-            col_mat[...], row_mat[:, pl.ds(base, TILE)], preferred_element_type=f32
-        )
-        kernel = jnp.exp(exponent).astype(bf16)
-        sums = jnp.dot(dir_mat[...], kernel, preferred_element_type=f32)
-        for j in range(TILE // LANES):
-            k = tile * (TILE // LANES) + j
-            task = rows_ref[k, TASK_AT:DIR_AT, :][0:1].astype(f32)
-            cov = jnp.zeros((LEVELS, LANES), f32)
-            for level in range(LEVELS):
-                cov = cov + jnp.where(task == float(level), cov_ref[:, level : level + 1], 0.0)
-            total = jnp.zeros((PROBES, LANES), f32)
-            for level in range(LEVELS):
-                part = sums[level * PROBES : (level + 1) * PROBES, j * LANES : (j + 1) * LANES]
-                total = total + cov[level : level + 1, :] * part
-            out_ref[k] = total
-        return carry
-
-    lax.fori_loop(0, n_rows * LANES // TILE, step, 0)
+    exponent = jnp.dot(col_mat[...], row_mat[...], preferred_element_type=f32)
+    sums = jnp.dot(dir_mat[...], jnp.exp(exponent).astype(bf16), preferred_element_type=f32)
+    for k in range(n_rows):
+        task = rows_ref[k, FEATS:DEPTH, :].astype(f32)[ROW_TASK : ROW_TASK + 1]
+        cov = jnp.zeros((LEVELS, LANES), f32)
+        for level in range(LEVELS):
+            cov = cov + jnp.where(task == float(level), cov_ref[:, level : level + 1], 0.0)
+        total = jnp.zeros((PROBES, LANES), f32)
+        for level in range(LEVELS):
+            part = sums[level * PROBES : (level + 1) * PROBES, k * LANES : (k + 1) * LANES]
+            total = total + cov[level : level + 1, :] * part
+        out_ref[k] = total
 
 
 def product_kernel(parts_ref, dir_ref, res_ref, product_ref, stats_ref):
@@ -149,7 +121,7 @@
     row_send, col_send = call(
         pack_kernel,
         [
-            jax.ShapeDtypeStruct((ROW_ROWS, LANES), bf16),
+            jax.ShapeDtypeStruct((DEPTH, LANES), bf16),
             jax.ShapeDtypeStruct((line, COL_ROWS, LANES), bf16),
         ],
         4,
@@ -174,7 +146,7 @@
             pltpu.VMEM((line * LANES, DEPTH), bf16),
             pltpu.VMEM((LEVELS * PROBES, line * LANES), bf16),
         ],
-        limit=40,
+        limit=36,
     )(rows, cols, task_cov)
     parts = lax.all_to_all(partial, PLANE, 0, 0)
     product, stats = call(

time: 91 us -> 90.2 us (level)
  no operation moved by 1% of the time
where the time goes in v5:
time: 90.2 us; the launch traced here: 89.5 us
  blocking collectives  63.3 us (70%)
  starting transfers between devices  15.9 us (18%)
  Pallas kernels  9.46 us (10%)
    all_gather x1, blocking collectives, body(): rows = lax.all_gather(row_send, PLANE)  26.2 us
    all_to_all x1, starting transfers between devices, body(): cols = lax.all_to_all(col_send, LINE, 0, 0, axis_index_groups=GATHER_ORDER)  15.9 us
    all_to_all x1, blocking collectives, body(): parts = lax.all_to_all(partial, PLANE, 0, 0)  13.8 us
    all_to_all x1, blocking collectives, body(): stats = lax.all_to_all(stats, LINE, 0, 0, axis_index_groups=SCALAR_ORDER)  12.8 us
    all_to_all x1, blocking collectives, body(): stats = jnp.sum(lax.all_to_all(stats, PLANE, 0, 0), axis=0)  10.4 us
    pallas_call x1, Pallas kernels, body(): call(block_kernel, jax.ShapeDtypeStruct((plane, PROBES, LANES), f32), 3,...  6.99 us
  transfers between devices with their start and end apart: 1, of which 0 were waited for; matrix products, arithmetic and copies ran while one was open for 0% of the time, Pallas kernels for 0%

profile of v5, /device:TPU:1, one launch (start us, length us, event | category | flops | bytes accessed | tf_op | source)
XLA Modules:
  0.0 89.5 jit_solution(11616339520061791460)
XLA Ops:
  0.6 1.6 %shard_map.94 = (bf16[80,128]{1,0:T(8,128)(2,1)}, bf16[16,88,128]{2,1,0:T(8,128)(2,1)}) custom-call(bf16[64,128]{1,0:T(8,128)(2,1)} %bitcast.17, f32[1,64]{1,0:T(1,128)} %bitcast.18, s32[1,128]{1,0:T(1,128)} %bitcast.19, f32[16,128]{1,0:T(8,128)} %bitcast.11), custom_call_target="tpu_custom_call" | custom-call | tf_op jit(solution)/shard_map/pallas_call | solution.py:121
  2.3 0.0 copy-start.4
  2.3 15.9 %all-to-all-start = ((bf16[16,88,128]{2,1,0:T(8,128)(2,1)}), bf16[16,88,128]{2,1,0:T(8,128)(2,1)S(1)}, u32[]{:S(2)}, u32[]{:S(2)}) async-start(bf16[16,88,128]{2,1,0:T(8,128)(2,1)} %get-tuple-element.11), calls=%async_computation | async-start | bytes 720896 | tf_op jit(solution)/shard_map/all_to_all | solution.py:138
  18.2 0.0 copy-done.4
  18.2 0.0 copy-start.3
  18.2 26.2 %all-gather = bf16[2560,128]{1,0:T(8,128)(2,1)S(1)} all-gather(bf16[80,128]{1,0:T(8,128)(2,1)S(1)} %copy-done.4), channel_id=2, replica_groups=mesh['z'=16,'x'=4,'y'=4,'core'=2] {'x','y','core'}, dimensions={0}, use_global_device_ids=true | all-gather | bytes 675840 | tf_op jit(solution)/shard_map/all_gather | solution.py:139
  44.5 0.0 all-to-all-done.cols_ref
  44.5 0.0 copy-done.3
  44.5 7.0 %shard_map.95 = f32[32,16,128]{2,1,0:T(8,128)S(1)} custom-call(bf16[32,80,128]{2,1,0:T(8,128)(2,1)S(1)} %bitcast.10, bf16[16,88,128]{2,1,0:T(8,128)(2,1)S(1)} %all-to-all-done.cols_ref, f32[8,8]{1,0:T(8,128)S(1)} %copy-done.3), custom_call_target="tpu_custom_call" | custom-call | tf_op jit(solution)/shard_map/pallas_call | solution.py:140
  51.5 0.0 copy-start
  51.5 0.0 copy-start.1
  51.5 13.8 %all_to_all.20.parts_ref = f32[32,16,128]{2,1,0:T(8,128)S(1)} all-to-all(f32[32,16,128]{2,1,0:T(8,128)S(1)} %shard_map.95), channel_id=1, replica_groups=mesh['z'=16,'x'=4,'y'=4,'core'=2] {'x','y','core'}, dimensions={0} | all-to-all | bytes 524288 | tf_op jit(solution)/shard_map/all_to_all | solution.py:151
  65.4 0.0 copy-done
  65.4 0.0 copy-done.1
  65.4 0.1 shard_map.96
  65.5 10.4 %all_to_all.21 = f32[32,1,128]{2,1,0:T(1,128)S(1)} all-to-all(f32[32,1,128]{2,1,0:T(1,128)S(1)} %get-tuple-element.12), channel_id=1, replica_groups=mesh['z'=16,'x'=4,'y'=4,'core'=2] {'x','y','core'}, dimensions={0} | all-to-all | bytes 32768 | tf_op jit(solution)/shard_map/all_to_all | solution.py:160
  75.9 0.1 reduce_sum.9
  76.0 0.0 copy-start.2
  76.0 12.8 %all_to_all.22.stats_ref = f32[16,1,128]{2,1,0:T(1,128)S(1)} all-to-all(f32[16,1,128]{2,1,0:T(1,128)S(1)} %broadcast_in_dim.14), channel_id=1, replica_groups={{256,288,320,352,384,416,448,480,0,32,64,96,128,160,192,224},{257,289,3..., dimensions={0} | all-to-all | bytes 16384 | tf_op jit(solution)/shard_map/all_to_all | solution.py:162
  88.8 0.0 copy-done.2
  88.8 0.7 shard_map.97
  (1 shorter events, 0.0 us)
Async XLA Ops:
  2.3 16.0 %copy-start.4 = (bf16[80,128]{1,0:T(8,128)(2,1)S(1)}, bf16[80,128]{1,0:T(8,128)(2,1)}, u32[]{:S(2)}) copy-start(bf16[80,128]{1,0:T(8,128)(2,1)} %get-tuple-element.10) | copy-start | bytes 61444
  2.3 42.2 %all-to-all-start = ((bf16[16,88,128]{2,1,0:T(8,128)(2,1)}), bf16[16,88,128]{2,1,0:T(8,128)(2,1)S(1)}, u32[]{:S(2)}, u32[]{:S(2)}) async-start(bf16[16,88,128]{2,1,0:T(8,128)(2,1)} %get-tuple-element.11), calls=%async_computation | async-start | bytes 720896 | tf_op jit(solution)/shard_map/all_to_all | solution.py:138
  18.2 26.3 %copy-start.3 = (f32[8,8]{1,0:T(8,128)S(1)}, f32[8,8]{1,0:T(8,128)}, u32[]{:S(2)}) copy-start(f32[8,8]{1,0:T(8,128)} %cov_ref.1) | copy-start | bytes 772
  51.5 13.9 %copy-start = (f32[128,16]{0,1:T(8,128)S(1)}, f32[128,16]{0,1:T(8,128)}, u32[]{:S(2)}) copy-start(f32[128,16]{0,1:T(8,128)} %param.13) | copy-start | bytes 24580
  51.5 13.9 %copy-start.1 = (f32[128,16]{0,1:T(8,128)S(1)}, f32[128,16]{0,1:T(8,128)}, u32[]{:S(2)}) copy-start(f32[128,16]{0,1:T(8,128)} %param.12) | copy-start | bytes 24580
  76.0 12.8 %copy-start.2 = (f32[128,16]{0,1:T(8,128)S(1)}, f32[128,16]{0,1:T(8,128)}, u32[]{:S(2)}) copy-start(f32[128,16]{0,1:T(8,128)} %param.11) | copy-start | bytes 24580

commit v6 on v5

--- a/solution.py
+++ b/solution.py
@@ -56,7 +56,7 @@
         row_mat[:, k * LANES : (k + 1) * LANES] = rows_ref[k]
     for k in range(n_cols):
         at = pl.ds(k * LANES, LANES)
-        col_mat[at, :] = cols_ref[k, :DEPTH, :].astype(f32).T.astype(bf16)
+        col_mat[at, :] = cols_ref[k, :DEPTH, :].T
         task = cols_ref[k, FEATS:DIR_AT, :].astype(f32)[COL_TASK : COL_TASK + 1]
         dirs = cols_ref[k, DIR_AT:, :].astype(f32)
         dir_mat[:, at] = jnp.concatenate(

time: 90.2 us -> 90.1 us (level)
  no operation moved by 1% of the time
where the time goes in v6:
time: 90.1 us; the launch traced here: 89.5 us
  blocking collectives  63.3 us (70%)
  starting transfers between devices  15.9 us (18%)
  Pallas kernels  9.4 us (10%)
    all_gather x1, blocking collectives, body(): rows = lax.all_gather(row_send, PLANE)  26.2 us
    all_to_all x1, starting transfers between devices, body(): cols = lax.all_to_all(col_send, LINE, 0, 0, axis_index_groups=GATHER_ORDER)  15.9 us
    all_to_all x1, blocking collectives, body(): parts = lax.all_to_all(partial, PLANE, 0, 0)  13.8 us
    all_to_all x1, blocking collectives, body(): stats = lax.all_to_all(stats, LINE, 0, 0, axis_index_groups=SCALAR_ORDER)  12.8 us
    all_to_all x1, blocking collectives, body(): stats = jnp.sum(lax.all_to_all(stats, PLANE, 0, 0), axis=0)  10.4 us
    pallas_call x1, Pallas kernels, body(): call(block_kernel, jax.ShapeDtypeStruct((plane, PROBES, LANES), f32), 3,...  6.92 us
  transfers between devices with their start and end apart: 1, of which 0 were waited for; matrix products, arithmetic and copies ran while one was open for 0% of the time, Pallas kernels for 0%

profile of v6, /device:TPU:1, one launch (start us, length us, event | category | flops | bytes accessed | tf_op | source)
XLA Modules:
  0.0 89.5 jit_solution(11103225352636129726)
XLA Ops:
  0.6 1.6 %shard_map.94 = (bf16[80,128]{1,0:T(8,128)(2,1)}, bf16[16,88,128]{2,1,0:T(8,128)(2,1)}) custom-call(bf16[64,128]{1,0:T(8,128)(2,1)} %bitcast.17, f32[1,64]{1,0:T(1,128)} %bitcast.18, s32[1,128]{1,0:T(1,128)} %bitcast.19, f32[16,128]{1,0:T(8,128)} %bitcast.11), custom_call_target="tpu_custom_call" | custom-call | tf_op jit(solution)/shard_map/pallas_call | solution.py:121
  2.3 0.0 copy-start.4
  2.3 15.9 %all-to-all-start = ((bf16[16,88,128]{2,1,0:T(8,128)(2,1)}), bf16[16,88,128]{2,1,0:T(8,128)(2,1)S(1)}, u32[]{:S(2)}, u32[]{:S(2)}) async-start(bf16[16,88,128]{2,1,0:T(8,128)(2,1)} %get-tuple-element.11), calls=%async_computation | async-start | bytes 720896 | tf_op jit(solution)/shard_map/all_to_all | solution.py:138
  18.2 0.0 copy-done.4
  18.2 0.0 copy-start.3
  18.2 26.2 %all-gather = bf16[2560,128]{1,0:T(8,128)(2,1)S(1)} all-gather(bf16[80,128]{1,0:T(8,128)(2,1)S(1)} %copy-done.4), channel_id=2, replica_groups=mesh['z'=16,'x'=4,'y'=4,'core'=2] {'x','y','core'}, dimensions={0}, use_global_device_ids=true | all-gather | bytes 675840 | tf_op jit(solution)/shard_map/all_gather | solution.py:139
  44.5 0.0 all-to-all-done.cols_ref
  44.5 0.0 copy-done.3
  44.5 6.9 %shard_map.95 = f32[32,16,128]{2,1,0:T(8,128)S(1)} custom-call(bf16[32,80,128]{2,1,0:T(8,128)(2,1)S(1)} %bitcast.10, bf16[16,88,128]{2,1,0:T(8,128)(2,1)S(1)} %all-to-all-done.cols_ref, f32[8,8]{1,0:T(8,128)S(1)} %copy-done.3), custom_call_target="tpu_custom_call" | custom-call | tf_op jit(solution)/shard_map/pallas_call | solution.py:140
  51.4 0.0 copy-start
  51.4 0.0 copy-start.1
  51.4 13.8 %all_to_all.20.parts_ref = f32[32,16,128]{2,1,0:T(8,128)S(1)} all-to-all(f32[32,16,128]{2,1,0:T(8,128)S(1)} %shard_map.95), channel_id=1, replica_groups=mesh['z'=16,'x'=4,'y'=4,'core'=2] {'x','y','core'}, dimensions={0} | all-to-all | bytes 524288 | tf_op jit(solution)/shard_map/all_to_all | solution.py:151
  65.3 0.0 copy-done
  65.3 0.0 copy-done.1
  65.3 0.1 shard_map.96
  65.4 10.4 %all_to_all.21 = f32[32,1,128]{2,1,0:T(1,128)S(1)} all-to-all(f32[32,1,128]{2,1,0:T(1,128)S(1)} %get-tuple-element.12), channel_id=1, replica_groups=mesh['z'=16,'x'=4,'y'=4,'core'=2] {'x','y','core'}, dimensions={0} | all-to-all | bytes 32768 | tf_op jit(solution)/shard_map/all_to_all | solution.py:160
  75.9 0.1 reduce_sum.9
  75.9 0.0 copy-start.2
  75.9 12.8 %all_to_all.22.stats_ref = f32[16,1,128]{2,1,0:T(1,128)S(1)} all-to-all(f32[16,1,128]{2,1,0:T(1,128)S(1)} %broadcast_in_dim.14), channel_id=1, replica_groups={{256,288,320,352,384,416,448,480,0,32,64,96,128,160,192,224},{257,289,3..., dimensions={0} | all-to-all | bytes 16384 | tf_op jit(solution)/shard_map/all_to_all | solution.py:162
  88.8 0.0 copy-done.2
  88.8 0.7 shard_map.97
  (1 shorter events, 0.0 us)
Async XLA Ops:
  2.3 16.0 %copy-start.4 = (bf16[80,128]{1,0:T(8,128)(2,1)S(1)}, bf16[80,128]{1,0:T(8,128)(2,1)}, u32[]{:S(2)}) copy-start(bf16[80,128]{1,0:T(8,128)(2,1)} %get-tuple-element.10) | copy-start | bytes 61444
  2.3 42.2 %all-to-all-start = ((bf16[16,88,128]{2,1,0:T(8,128)(2,1)}), bf16[16,88,128]{2,1,0:T(8,128)(2,1)S(1)}, u32[]{:S(2)}, u32[]{:S(2)}) async-start(bf16[16,88,128]{2,1,0:T(8,128)(2,1)} %get-tuple-element.11), calls=%async_computation | async-start | bytes 720896 | tf_op jit(solution)/shard_map/all_to_all | solution.py:138
  18.2 26.3 %copy-start.3 = (f32[8,8]{1,0:T(8,128)S(1)}, f32[8,8]{1,0:T(8,128)}, u32[]{:S(2)}) copy-start(f32[8,8]{1,0:T(8,128)} %cov_ref.1) | copy-start | bytes 772
  51.4 13.9 %copy-start = (f32[128,16]{0,1:T(8,128)S(1)}, f32[128,16]{0,1:T(8,128)}, u32[]{:S(2)}) copy-start(f32[128,16]{0,1:T(8,128)} %param.13) | copy-start | bytes 24580
  51.4 13.9 %copy-start.1 = (f32[128,16]{0,1:T(8,128)S(1)}, f32[128,16]{0,1:T(8,128)}, u32[]{:S(2)}) copy-start(f32[128,16]{0,1:T(8,128)} %param.12) | copy-start | bytes 24580
  75.9 12.8 %copy-start.2 = (f32[128,16]{0,1:T(8,128)S(1)}, f32[128,16]{0,1:T(8,128)}, u32[]{:S(2)}) copy-start(f32[128,16]{0,1:T(8,128)} %param.11) | copy-start | bytes 24580
